TPU v7x, 32 devices: a whole 2x2x4 slice. The times are simulated.
32 devices in a mesh: tm: 4 (over y, x), stat: 8 (over z, core).
Axes of the slice: x: 2, y: 2, z: 4, core: 2. Of those that a mesh axis runs over, the one named last changes fastest.
Arguments:
- voltages: bfloat16 [512, 163840], P('stat', 'tm'), may hold values from -6 to 6
- taper: float32 [16, 4096], replicated, may hold values from -1.5 to 1.5
Outputs:
- visibility: float32 [4, 2, 512, 5, 64, 512], P('tm', None, 'stat')
All inputs are finite; a program needn't handle non-finite values.
Results may differ from a plain program's by a relative error of at most 0.0039.
Values may be sent and summed in bfloat16 or wider, within the bound.
A program may use at most 512 MiB of HBM per device.

v0:
```python
import math
import jax
import jax.numpy as jnp
from jax import lax
from jax.sharding import PartitionSpec as P

NSPEC = 25


def from_behind(value, axis, steps):
    count = lax.axis_size(axis)
    pairs = [(source, (source + steps) % count) for source in range(count)]
    return lax.ppermute(value, axis, pairs)


def dft_table(segment, channel_count, frame_len):
    sample_idx = jnp.arange(segment, dtype=jnp.int32)[:, None]
    channel_idx = jnp.arange(channel_count, dtype=jnp.int32)[None, :]
    angles = 2.0 * math.pi / segment * (sample_idx * channel_idx % segment).astype(jnp.float32)
    cosine = jnp.cos(angles)
    sine_part = jnp.sin(angles)
    upper = jnp.concatenate([cosine, -sine_part], axis=1)
    lower = jnp.concatenate([sine_part, cosine], axis=1)
    return jnp.concatenate([upper, lower], axis=0) / math.sqrt(frame_len)


def fold_twiddle(filtered, residue, tm_count, frame_len):
    row_count = filtered.shape[0]
    segment = frame_len // tm_count
    pieces = filtered.reshape(row_count, tm_count, segment)
    outer_idx = jnp.arange(tm_count, dtype=jnp.int32)
    outer_angles = 2.0 * math.pi / tm_count * (residue * outer_idx % tm_count).astype(jnp.float32)
    sum_real = jnp.sum(pieces * jnp.cos(outer_angles)[None, :, None], axis=1)
    sum_imag = -jnp.sum(pieces * jnp.sin(outer_angles)[None, :, None], axis=1)
    inner_idx = jnp.arange(segment, dtype=jnp.int32)
    inner_angles = 2.0 * math.pi / frame_len * (residue * inner_idx % frame_len).astype(jnp.float32)
    inner_cos = jnp.cos(inner_angles)[None, :]
    inner_sin = jnp.sin(inner_angles)[None, :]
    twisted_real = sum_real * inner_cos + sum_imag * inner_sin
    twisted_imag = sum_imag * inner_cos - sum_real * inner_sin
    return jnp.concatenate([twisted_real, twisted_imag], axis=1)


def polyphase(series, taper, spectra_count):
    row_count = series.shape[0]
    tap_count = taper.shape[0]
    frame_len = taper.shape[1]
    frames = series.reshape(row_count, spectra_count + tap_count - 1, frame_len)
    filtered = jnp.zeros((row_count, spectra_count, frame_len), jnp.float32)
    for tap_index in range(tap_count):
        filtered = filtered + taper[tap_index][None, None, :] * frames[
            :, tap_index : tap_index + spectra_count, :
        ].astype(jnp.float32)
    return filtered.reshape(row_count * spectra_count, frame_len)


def correlate(conjugated, partner_block, spectra_count):
    cross = jnp.einsum(
        "opisc,pmsc->oimc", conjugated, partner_block, preferred_element_type=jnp.float32
    )
    return cross / spectra_count


def shards(voltages, taper):
    tm_count = lax.axis_size("tm")
    stat_count = lax.axis_size("stat")
    tm_index = lax.axis_index("tm")
    local_inputs = voltages.shape[0]
    frame_len = taper.shape[1]
    segment = frame_len // tm_count
    channel_count = frame_len // 2 // tm_count
    spectra_count = NSPEC
    lag_count = stat_count // 2 + 1
    table = dft_table(segment, channel_count, frame_len)
    whole_series = lax.all_gather(voltages, "tm", axis=1, tiled=True)
    filtered = polyphase(whole_series, taper, spectra_count)
    twisted = fold_twiddle(filtered, tm_index, tm_count, frame_len)
    spectra = jnp.dot(
        twisted, table, precision=lax.Precision.HIGHEST, preferred_element_type=jnp.float32
    )
    spectra = spectra.reshape(local_inputs, spectra_count, 2, channel_count)
    own_block = jnp.transpose(spectra, (2, 0, 1, 3)).astype(jnp.bfloat16)
    conjugated = jnp.stack([own_block, jnp.stack([own_block[1], -own_block[0]])])
    visibility = jnp.zeros((2, local_inputs, lag_count, local_inputs, channel_count), jnp.float32)
    visibility = visibility.at[:, :, 0].set(correlate(conjugated, own_block, spectra_count))

    def lag_step(lag_index, carried):
        partner_block, accumulated = carried
        partner_block = from_behind(partner_block, "stat", -1)
        cross = correlate(conjugated, partner_block, spectra_count)
        accumulated = lax.dynamic_update_slice_in_dim(accumulated, cross[:, :, None], lag_index, 2)
        return (partner_block, accumulated)

    carried_out = lax.fori_loop(1, lag_count, lag_step, (own_block, visibility))
    visibility = carried_out[1]
    return visibility[None]


def solution(mesh):
    return jax.shard_map(
        shards,
        mesh=mesh,
        in_specs=(P("stat", "tm"), P()),
        out_specs=P("tm", None, "stat", None, None, None),
        check_vma=False,
    )
```

profile of v0, /device:TPU:0, one launch (start us, length us, event | category | flops | bytes accessed | tf_op | source)
XLA Modules:
  0.0 1070.2 jit_solution(5715505198837523400)
XLA Ops:
  6.5 0.0 all-gather.2.cloned.1.call-start
  6.5 0.7 all-gather.2.cloned.1.call-update
  7.3 0.1 fusion.36
  7.3 0.1 fusion.31
  7.4 7.7 fusion.24
  15.1 9.3 fusion.22
  24.3 2.3 fusion.41
  26.6 178.4 %all-gather.2.cloned.1.call-done = bf16[64,163840]{1,0:T(8,128)(2,1)} async-done(((bf16[64,40960]{1,0:T(8,128)(2,1)}), bf16[64,163840]{1,0:T(8,128)(2,1)}) %all-gather.2.cloned.1.call-update) | async-done | bytes 20971536 | tf_op jit(solution)/shard_map/all_gather | solution.py:75
  205.0 22.7 %copy.22 = bf16[8,8,40,4096]{3,2,1,0:T(8,128)(2,1)} copy(bf16[8,8,40,4096]{3,1,2,0:T(8,128)(2,1)} %bitcast.68) | data formatting | bytes 41943040
  227.7 134.3 %multiply_add_fusion = f32[64,25,4096]{2,1,0:T(8,128)} fusion(bf16[64,40,4096]{2,1,0:T(8,128)(2,1)} %bitcast.66, f32[4096]{0:T(1024)S(1)} %bitcast.83, f32[4096]{0:T(1024)S(1)} %bitcast.84, f32[4096]{0:T(1024)S(1)} %bitcast.70, f32[4096]{0:T(1024)S(1)} %bitcast.71, f32[4096]{0:T(1024)S(1)} %bitcast.72, f32[4096]{0:T(1024)S(1)} %bitcast.73, ...), kind=kLoop, calls=%fused_computation.4 | loop fusion | flops 308019200 | bytes 236191744 | tf_op jit(solution)/shard_map/add | solution.py:51
  362.0 31.6 %reshape_reshape.3 = f32[1600,4,1024]{2,1,0:T(4,128)} reshape(f32[64,25,4096]{2,1,0:T(8,128)} %multiply_add_fusion) | data formatting | bytes 52428800 | tf_op jit(solution)/shard_map/reshape;reshape | solution.py:30
  393.6 45.7 %multiply_reduce_fusion = (f32[1600,1024]{1,0:T(8,128)}, f32[1600,1024]{1,0:T(8,128)}) fusion(f32[1600,4,1024]{2,1,0:T(4,128)} %reshape_reshape.3, f32[4]{0:T(128)S(1)} %get-tuple-element.166, f32[4]{0:T(128)S(1)} %get-tuple-element.167), kind=kLoop, calls=%fused_computation.5 | loop fusion | flops 22937600 | bytes 39321632 | tf_op jit(solution)/shard_map/reduce_sum | solution.py:34
  439.2 12.9 %multiply_add_fusion.1 = (f32[1600,1024]{1,0:T(8,128)}, f32[1600,1024]{1,0:T(8,128)}) fusion(f32[1600,1024]{1,0:T(8,128)} %get-tuple-element.133, f32[1600,1024]{1,0:T(8,128)} %get-tuple-element.132, f32[1024]{0:T(1024)S(1)} %get-tuple-element.164, f32[1024]{0:T(1024)S(1)} %get-tuple-element.165), kind=kLoop, calls=%fused_computation.21 | loop fusion | flops 11468800 | bytes 26222592 | tf_op jit(solution)/shard_map/add | solution.py:39
  452.1 48.8 %fusion.13 = bf16[1600,1024]{1,0:T(8,128)(2,1)} fusion(f32[1024,512]{1,0:T(8,128)} %get-tuple-element.169, f32[1024,512]{1,0:T(8,128)} %get-tuple-element.168, f32[1024,512]{1,0:T(8,128)S(1)} %fusion.24, f32[1600,1024]{1,0:T(8,128)} %get-tuple-element.143, f32[1600,1024]{1,0:T(8,128)} %get-tuple-element.142), kind=kOutput, calls=%fused_computation.23 | convolution fusion | flops 40278622208 | bytes 22675456 | tf_op jit(solution)/shard_map/dot_general | solution.py:78
  501.0 7.4 convert_element_type.106
  508.3 2.4 copy.25
  510.7 13.2 %copy.21 = bf16[64,25,2,512]{0,1,2,3:T(8,128)(2,1)} copy(bf16[64,25,2,512]{3,2,1,0:T(2,128)(2,1)S(1)} %convert_element_type.106) | data formatting | bytes 6553600 | tf_op jit(solution)/shard_map/convert_element_type | solution.py:82
  523.9 2.1 fusion.40
  526.0 0.3 maximum_bitcast_fusion
  526.3 5.3 pad_maximum_fusion
  531.7 23.9 %copy.12 = bf16[2,2,64,25,512]{2,3,1,0,4:T(8,128)(2,1)} copy(bf16[2,2,64,25,512]{4,2,3,1,0:T(8,128)(2,1)} %pad_maximum_fusion) | data formatting | bytes 13107200 | tf_op jit(solution)/shard_map/stack | solution.py:83
  555.6 20.9 %fusion = f32[2,64,1,64,512]{1,3,0,4,2:T(8,128)} fusion(bf16[2,2,64,25,512]{2,3,1,0,4:T(8,128)(2,1)} %copy.12, bf16[64,25,2,512]{0,1,2,3:T(8,128)(2,1)} %copy.21), kind=kOutput, calls=%fused_computation.3 | convolution fusion | flops 423624704 | bytes 26607616 | tf_op jit(solution)/shard_map/opisc,pmsc->oimc/dot_general | solution.py:58
  576.5 63.0 %scatter.4 = f32[2,64,5,64,512]{1,3,0,4,2:T(8,128)} pad(f32[2,64,1,64,512]{1,3,0,4,2:T(8,128)} %fusion, f32[]{:T(128)} %constant.126.clone.1), padding=0_0x0_0x0_4x0_0x0_0 | pad | bytes 100663296 | tf_op jit(solution)/shard_map/scatter | solution.py:85
  639.5 298.8 %while.18 = (s32[]{:T(128)}, bf16[2,64,25,512]{3,1,2,0:T(8,128)(2,1)}, f32[2,64,5,64,512]{1,3,0,4,2:T(8,128)}, bf16[2,2,64,25,512]{2,3,1,0,4:T(8,128)(2,1)}, s32[]{:T(128)}, /*index=5*/s32[]{:T(128)}, s32[]{:T(128)}) while((s32[]{:T(128)}, bf16[2,64,25,512]{3,1,2,0:T(8,128)(2,1)}, f32[2,64,5,64,512]{1,3,0,4,2:T(8,128)}, ...), condition=%wide.region_3.4_spmd, body=%wide.region_2.3_spmd.sunk | while | flops 423624704 | bytes 84934808 | solution.py:94
  639.5 2.8 collective-permute-start
  642.3 36.5 %collective-permute-done = bf16[2,64,25,512]{3,1,2,0:T(8,128)(2,1)S(1)} collective-permute-done((bf16[2,64,25,512]{3,1,2,0:T(8,128)(2,1)}, bf16[2,64,25,512]{3,1,2,0:T(8,128)(2,1)S(1)}, u32[]{:S(2)}, u32[]{:S(2)}) %collective-permute-start) | collective-permute-done | bytes 3276832 | tf_op jit(solution)/shard_map/while/body/eval_jaxpr/ppermute | solution.py:13
  678.8 12.5 %copy.27 = bf16[2,64,25,512,1]{1,2,0,4,3:T(8,128)(2,1)} copy(bf16[2,64,25,512,1]{3,1,2,0,4:T(8,128)(2,1)S(1)} %bitcast.67) | data formatting | bytes 6553600 | tf_op jit(solution)/shard_map/while/body/eval_jaxpr/ppermute | solution.py:13
  691.2 20.7 %bitcast_dynamic-update-slice_fusion.2 = f32[2,64,5,64,512]{1,3,0,4,2:T(8,128)} fusion(f32[2,64,5,64,512]{1,3,0,4,2:T(8,128)} %get-tuple-element.204, s32[]{:T(128)S(6)} %select_n.82, bf16[2,64,25,512,1]{1,2,0,4,3:T(8,128)(2,1)} %copy.27, bf16[2,2,64,25,512]{2,3,1,0,4:T(8,128)(2,1)} %get-tuple-element.212), kind=kOutput, calls=%fused_computation.clone.1 | convolution fusion | flops 423624704 | bytes 58720260 | tf_op jit(solution)/shard_map/while/body/eval_jaxpr/opisc,pmsc->oimc/dot_general | solution.py:58
  711.9 1.7 copy.36
  713.5 3.6 collective-permute-start
  717.1 36.5 %collective-permute-done = bf16[2,64,25,512]{3,1,2,0:T(8,128)(2,1)S(1)} collective-permute-done((bf16[2,64,25,512]{3,1,2,0:T(8,128)(2,1)}, bf16[2,64,25,512]{3,1,2,0:T(8,128)(2,1)S(1)}, u32[]{:S(2)}, u32[]{:S(2)}) %collective-permute-start) | collective-permute-done | bytes 3276832 | tf_op jit(solution)/shard_map/while/body/eval_jaxpr/ppermute | solution.py:13
  753.6 12.5 %copy.27 = bf16[2,64,25,512,1]{1,2,0,4,3:T(8,128)(2,1)} copy(bf16[2,64,25,512,1]{3,1,2,0,4:T(8,128)(2,1)S(1)} %bitcast.67) | data formatting | bytes 6553600 | tf_op jit(solution)/shard_map/while/body/eval_jaxpr/ppermute | solution.py:13
  766.1 20.7 %bitcast_dynamic-update-slice_fusion.2 = f32[2,64,5,64,512]{1,3,0,4,2:T(8,128)} fusion(f32[2,64,5,64,512]{1,3,0,4,2:T(8,128)} %get-tuple-element.204, s32[]{:T(128)S(6)} %select_n.82, bf16[2,64,25,512,1]{1,2,0,4,3:T(8,128)(2,1)} %copy.27, bf16[2,2,64,25,512]{2,3,1,0,4:T(8,128)(2,1)} %get-tuple-element.212), kind=kOutput, calls=%fused_computation.clone.1 | convolution fusion | flops 423624704 | bytes 58720260 | tf_op jit(solution)/shard_map/while/body/eval_jaxpr/opisc,pmsc->oimc/dot_general | solution.py:58
  786.8 1.7 copy.36
  788.5 3.6 collective-permute-start
  792.1 36.5 %collective-permute-done = bf16[2,64,25,512]{3,1,2,0:T(8,128)(2,1)S(1)} collective-permute-done((bf16[2,64,25,512]{3,1,2,0:T(8,128)(2,1)}, bf16[2,64,25,512]{3,1,2,0:T(8,128)(2,1)S(1)}, u32[]{:S(2)}, u32[]{:S(2)}) %collective-permute-start) | collective-permute-done | bytes 3276832 | tf_op jit(solution)/shard_map/while/body/eval_jaxpr/ppermute | solution.py:13
  828.6 12.5 %copy.27 = bf16[2,64,25,512,1]{1,2,0,4,3:T(8,128)(2,1)} copy(bf16[2,64,25,512,1]{3,1,2,0,4:T(8,128)(2,1)S(1)} %bitcast.67) | data formatting | bytes 6553600 | tf_op jit(solution)/shard_map/while/body/eval_jaxpr/ppermute | solution.py:13
  841.1 20.6 %bitcast_dynamic-update-slice_fusion.2 = f32[2,64,5,64,512]{1,3,0,4,2:T(8,128)} fusion(f32[2,64,5,64,512]{1,3,0,4,2:T(8,128)} %get-tuple-element.204, s32[]{:T(128)S(6)} %select_n.82, bf16[2,64,25,512,1]{1,2,0,4,3:T(8,128)(2,1)} %copy.27, bf16[2,2,64,25,512]{2,3,1,0,4:T(8,128)(2,1)} %get-tuple-element.212), kind=kOutput, calls=%fused_computation.clone.1 | convolution fusion | flops 423624704 | bytes 58720260 | tf_op jit(solution)/shard_map/while/body/eval_jaxpr/opisc,pmsc->oimc/dot_general | solution.py:58
  861.7 1.7 copy.36
  863.4 3.6 collective-permute-start
  867.0 36.5 %collective-permute-done = bf16[2,64,25,512]{3,1,2,0:T(8,128)(2,1)S(1)} collective-permute-done((bf16[2,64,25,512]{3,1,2,0:T(8,128)(2,1)}, bf16[2,64,25,512]{3,1,2,0:T(8,128)(2,1)S(1)}, u32[]{:S(2)}, u32[]{:S(2)}) %collective-permute-start) | collective-permute-done | bytes 3276832 | tf_op jit(solution)/shard_map/while/body/eval_jaxpr/ppermute | solution.py:13
  903.5 12.5 %copy.27 = bf16[2,64,25,512,1]{1,2,0,4,3:T(8,128)(2,1)} copy(bf16[2,64,25,512,1]{3,1,2,0,4:T(8,128)(2,1)S(1)} %bitcast.67) | data formatting | bytes 6553600 | tf_op jit(solution)/shard_map/while/body/eval_jaxpr/ppermute | solution.py:13
  915.9 20.7 %bitcast_dynamic-update-slice_fusion.2 = f32[2,64,5,64,512]{1,3,0,4,2:T(8,128)} fusion(f32[2,64,5,64,512]{1,3,0,4,2:T(8,128)} %get-tuple-element.204, s32[]{:T(128)S(6)} %select_n.82, bf16[2,64,25,512,1]{1,2,0,4,3:T(8,128)(2,1)} %copy.27, bf16[2,2,64,25,512]{2,3,1,0,4:T(8,128)(2,1)} %get-tuple-element.212), kind=kOutput, calls=%fused_computation.clone.1 | convolution fusion | flops 423624704 | bytes 58720260 | tf_op jit(solution)/shard_map/while/body/eval_jaxpr/opisc,pmsc->oimc/dot_general | solution.py:58
  936.6 1.7 copy.36
  938.2 124.9 %copy.14 = f32[2,64,5,64,512]{4,3,2,1,0:T(8,128)} copy(f32[2,64,5,64,512]{1,3,0,4,2:T(8,128)} %get-tuple-element.127) | data formatting | bytes 167772160 | tf_op jit(solution)/shard_map/while | solution.py:94
Async XLA Ops:
  6.5 198.5 %all-gather.2.cloned.1.call-start = ((), (), s32[]{:S(2)}) async-start(), calls=%async_computation | async-start | bytes 26214400 | tf_op jit(solution)/shard_map/all_gather | solution.py:75
  639.5 39.3 %collective-permute-start = (bf16[2,64,25,512]{3,1,2,0:T(8,128)(2,1)}, bf16[2,64,25,512]{3,1,2,0:T(8,128)(2,1)S(1)}, u32[]{:S(2)}, u32[]{:S(2)}) collective-permute-start(bf16[2,64,25,512]{3,1,2,0:T(8,128)(2,1)} %get-tuple-element.203), channel_id=1, source_target_pairs={{0,7},{1,0},{2,1},{3,2},{4,3},{5,4},{6,5},{7,6},{8,15},{9,8},{10,9... | collective-permute-start | bytes 9830408 | tf_op jit(solution)/shard_map/while/body/eval_jaxpr/ppermute | solution.py:13
  713.5 40.1 %collective-permute-start = (bf16[2,64,25,512]{3,1,2,0:T(8,128)(2,1)}, bf16[2,64,25,512]{3,1,2,0:T(8,128)(2,1)S(1)}, u32[]{:S(2)}, u32[]{:S(2)}) collective-permute-start(bf16[2,64,25,512]{3,1,2,0:T(8,128)(2,1)} %get-tuple-element.203), channel_id=1, source_target_pairs={{0,7},{1,0},{2,1},{3,2},{4,3},{5,4},{6,5},{7,6},{8,15},{9,8},{10,9... | collective-permute-start | bytes 9830408 | tf_op jit(solution)/shard_map/while/body/eval_jaxpr/ppermute | solution.py:13
  788.5 40.1 %collective-permute-start = (bf16[2,64,25,512]{3,1,2,0:T(8,128)(2,1)}, bf16[2,64,25,512]{3,1,2,0:T(8,128)(2,1)S(1)}, u32[]{:S(2)}, u32[]{:S(2)}) collective-permute-start(bf16[2,64,25,512]{3,1,2,0:T(8,128)(2,1)} %get-tuple-element.203), channel_id=1, source_target_pairs={{0,7},{1,0},{2,1},{3,2},{4,3},{5,4},{6,5},{7,6},{8,15},{9,8},{10,9... | collective-permute-start | bytes 9830408 | tf_op jit(solution)/shard_map/while/body/eval_jaxpr/ppermute | solution.py:13
  863.4 40.1 %collective-permute-start = (bf16[2,64,25,512]{3,1,2,0:T(8,128)(2,1)}, bf16[2,64,25,512]{3,1,2,0:T(8,128)(2,1)S(1)}, u32[]{:S(2)}, u32[]{:S(2)}) collective-permute-start(bf16[2,64,25,512]{3,1,2,0:T(8,128)(2,1)} %get-tuple-element.203), channel_id=1, source_target_pairs={{0,7},{1,0},{2,1},{3,2},{4,3},{5,4},{6,5},{7,6},{8,15},{9,8},{10,9... | collective-permute-start | bytes 9830408 | tf_op jit(solution)/shard_map/while/body/eval_jaxpr/ppermute | solution.py:13
Sparse Core Ops, SparseCore 0:
  9.2 195.7 all-gather.1
where the time goes:
time: 1080 us; the launch traced here: 1070 us
  local copies, waits for them, and re-layouts  348 us (32%)
  waiting for transfers between devices  325 us (30%)
  other arithmetic  218 us (20%)
  matrix products  152 us (14%)
  starting transfers between devices  13.6 us (1%)
  between operations  13.6 us (1%)
    all_gather x1, waiting for transfers between devices, shards(): whole_series = lax.all_gather(voltages, 'tm', axis=1, tiled=True)  178 us
    ppermute x4, waiting for transfers between devices, from_behind(): return lax.ppermute(value, axis, pairs)  146 us
    add x1, other arithmetic, polyphase(): filtered + taper[tap_index][None, None, :] * frames[:, tap_index:tap_inde...  134 us
    while x1, local copies, waits for them, and re-layouts, shards(): carried_out = lax.fori_loop(1, lag_count, lag_step, (own_block, visibility))  125 us
    dot_general x5, matrix products, correlate(): jnp.einsum('opisc,pmsc->oimc', conjugated, partner_block, preferred_eleme...  104 us
    scatter x1, local copies, waits for them, and re-layouts, shards(): visibility.at[:, :, 0].set(correlate(conjugated, own_block, spectra_count))  63 us
    ppermute x4, local copies, waits for them, and re-layouts, from_behind(): return lax.ppermute(value, axis, pairs)  49.8 us
    dot_general x1, matrix products, shards(): jnp.dot(twisted, table, precision=lax.Precision.HIGHEST, preferred_elemen...  48.8 us
  transfers between devices with their start and end apart: 5, of which 5 were waited for; matrix products, arithmetic and copies ran while one was open for 2% of the time, Pallas kernels for 0%

commit v1 on v0

--- a/solution.py
+++ b/solution.py
@@ -72,7 +72,22 @@
     spectra_count = NSPEC
     lag_count = stat_count // 2 + 1
     table = dft_table(segment, channel_count, frame_len)
-    whole_series = lax.all_gather(voltages, "tm", axis=1, tiled=True)
+    ways, here, step = (lax.axis_size("tm"), lax.axis_index("tm"), voltages.shape[1])
+    lengths = [n * ways if d == 1 else n for d, n in enumerate(voltages.shape)]
+    whole_series = lax.dynamic_update_slice_in_dim(
+        jnp.zeros(lengths, voltages.dtype), voltages, here * step, axis=1
+    )
+    going_up = going_down = voltages
+    for far in range(1, ways // 2 + 1):
+        going_up = lax.ppermute(going_up, "tm", [(d, (d + 1) % ways) for d in range(ways)])
+        whole_series = lax.dynamic_update_slice_in_dim(
+            whole_series, going_up, (here - far) % ways * step, axis=1
+        )
+        if 2 * far < ways:
+            going_down = lax.ppermute(going_down, "tm", [(d, (d - 1) % ways) for d in range(ways)])
+            whole_series = lax.dynamic_update_slice_in_dim(
+                whole_series, going_down, (here + far) % ways * step, axis=1
+            )
     filtered = polyphase(whole_series, taper, spectra_count)
     twisted = fold_twiddle(filtered, tm_index, tm_count, frame_len)
     spectra = jnp.dot(

time: 1080 us -> 1220 us (1.13)
  waiting for transfers between devices: 325 us -> 456 us
  other arithmetic: 218 us -> 233 us
  between operations: 13.6 us -> 0.33 us
    ppermute x0 -> x3, waiting for transfers between devices: none -> 310 us  [the longest x2 310 us: shards(): lax.ppermute(going_up, 'tm', [(d, (d + 1) % ways) for d in range(ways)])]
    all_gather x1 -> x0, waiting for transfers between devices: 178 us -> none  [shards(): whole_series = lax.all_gather(voltages, 'tm', axis=1, tiled=True)]
    dynamic_update_slice x0 -> x4, local copies, waits for them, and re-layouts: none -> 13.5 us  [the longest x2 6.75 us: shards(): lax.dynamic_update_slice_in_dim(whole_series, going_up, (here - far) % wa...]
  transfers between devices with their start and end apart: 5 -> 7, of which waited for: 5 -> 6; matrix products, arithmetic and copies ran while one was open for 2% -> 2% of each run, Pallas kernels for 0% -> 0%
where the time goes in v1:
time: 1220 us; the launch traced here: 1210 us
  waiting for transfers between devices  456 us (37%)
  local copies, waits for them, and re-layouts  351 us (29%)
  other arithmetic  233 us (19%)
  matrix products  152 us (12%)
  starting transfers between devices  17.4 us (1%)
    ppermute x2, waiting for transfers between devices, shards(): lax.ppermute(going_up, 'tm', [(d, (d + 1) % ways) for d in range(ways)])  310 us
    ppermute x4, waiting for transfers between devices, from_behind(): return lax.ppermute(value, axis, pairs)  146 us
    add x1, other arithmetic, polyphase(): filtered + taper[tap_index][None, None, :] * frames[:, tap_index:tap_inde...  137 us
    while x1, local copies, waits for them, and re-layouts, shards(): carried_out = lax.fori_loop(1, lag_count, lag_step, (own_block, visibility))  125 us
    dot_general x5, matrix products, correlate(): jnp.einsum('opisc,pmsc->oimc', conjugated, partner_block, preferred_eleme...  104 us
    scatter x1, local copies, waits for them, and re-layouts, shards(): visibility.at[:, :, 0].set(correlate(conjugated, own_block, spectra_count))  63 us
    reduce_sum x1, other arithmetic, fold_twiddle(): sum_imag = -jnp.sum(pieces * jnp.sin(outer_angles)[None, :, None], axis=1)  57.3 us
    ppermute x4, local copies, waits for them, and re-layouts, from_behind(): return lax.ppermute(value, axis, pairs)  49.8 us
  transfers between devices with their start and end apart: 7, of which 6 were waited for; matrix products, arithmetic and copies ran while one was open for 2% of the time, Pallas kernels for 0%

profile of v1, /device:TPU:0, one launch (start us, length us, event | category | flops | bytes accessed | tf_op | source)
XLA Modules:
  0.0 1209.6 jit_solution(11362124293809446201)
XLA Ops:
  0.0 3.9 collective-permute-start.2
  3.9 0.0 collective-permute-start.1
  3.9 0.1 fusion.36
  3.9 0.1 fusion.31
  4.0 8.6 fusion.24
  12.6 9.1 fusion.22
  21.7 0.0 copy-start.1
  21.7 1.5 broadcast_in_dim.23
  23.2 3.4 constant_dynamic-update-slice_fusion.3
  26.6 0.0 copy-done.1
  26.6 0.2 fusion.41
  26.8 203.0 %collective-permute-done.1 = bf16[64,40960]{1,0:T(8,128)(2,1)} collective-permute-done((bf16[64,40960]{1,0:T(8,128)(2,1)}, bf16[64,40960]{1,0:T(8,128)(2,1)}, u32[]{:S(2)}, u32[]{:S(2)}) %collective-permute-start.1) | collective-permute-done | bytes 5242912 | tf_op jit(solution)/shard_map/ppermute | solution.py:82
  229.9 1.5 collective-permute-start.3
  231.3 3.4 constant_dynamic-update-slice_fusion.2
  234.7 0.0 collective-permute-done.2
  234.8 3.4 constant_dynamic-update-slice_fusion.1
  238.1 106.9 %collective-permute-done.3 = bf16[64,40960]{1,0:T(8,128)(2,1)} collective-permute-done((bf16[64,40960]{1,0:T(8,128)(2,1)}, bf16[64,40960]{1,0:T(8,128)(2,1)}, u32[]{:S(2)}, u32[]{:S(2)}) %collective-permute-start.3) | collective-permute-done | bytes 5242912 | tf_op jit(solution)/shard_map/ppermute | solution.py:82
  345.0 3.4 constant_dynamic-update-slice_fusion
  348.3 13.6 %copy.22 = bf16[8,8,40,4096]{3,2,1,0:T(8,128)(2,1)} copy(bf16[8,8,40,4096]{3,1,2,0:T(8,128)(2,1)S(1)} %bitcast.68) | data formatting | bytes 41943040
  362.0 136.8 %multiply_add_fusion = f32[64,25,4096]{2,1,0:T(8,128)} fusion(bf16[64,40,4096]{2,1,0:T(8,128)(2,1)} %bitcast.66, f32[4096]{0:T(1024)S(1)} %bitcast.83, f32[4096]{0:T(1024)S(1)} %bitcast.84, f32[4096]{0:T(1024)S(1)} %bitcast.70, f32[4096]{0:T(1024)S(1)} %bitcast.71, f32[4096]{0:T(1024)S(1)} %bitcast.72, f32[4096]{0:T(1024)S(1)} %bitcast.73, ...), kind=kLoop, calls=%fused_computation.4 | loop fusion | flops 308019200 | bytes 236191744 | tf_op jit(solution)/shard_map/add | solution.py:51
  498.8 31.4 %reshape_reshape.3 = f32[1600,4,1024]{2,1,0:T(4,128)} reshape(f32[64,25,4096]{2,1,0:T(8,128)} %multiply_add_fusion) | data formatting | bytes 52428800 | tf_op jit(solution)/shard_map/reshape;reshape | solution.py:30
  530.1 57.3 %multiply_reduce_fusion = (f32[1600,1024]{1,0:T(8,128)}, f32[1600,1024]{1,0:T(8,128)}) fusion(f32[1600,4,1024]{2,1,0:T(4,128)} %reshape_reshape.3, f32[4]{0:T(128)S(1)} %get-tuple-element.164, f32[4]{0:T(128)S(1)} %get-tuple-element.165), kind=kLoop, calls=%fused_computation.5 | loop fusion | flops 22937600 | bytes 39321632 | tf_op jit(solution)/shard_map/reduce_sum | solution.py:34
  587.4 0.0 copy-start
  587.4 13.1 %multiply_add_fusion.1 = (f32[1600,1024]{1,0:T(8,128)}, f32[1600,1024]{1,0:T(8,128)}) fusion(f32[1600,1024]{1,0:T(8,128)} %get-tuple-element.133, f32[1600,1024]{1,0:T(8,128)} %get-tuple-element.132, f32[1024]{0:T(1024)S(1)} %get-tuple-element.166, f32[1024]{0:T(1024)S(1)} %get-tuple-element.167), kind=kLoop, calls=%fused_computation.21 | loop fusion | flops 11468800 | bytes 26222592 | tf_op jit(solution)/shard_map/add | solution.py:39
  600.5 0.0 copy-done
  600.5 48.5 %fusion.13 = bf16[1600,1024]{1,0:T(8,128)(2,1)} fusion(f32[1024,512]{1,0:T(8,128)} %get-tuple-element.169, f32[1024,512]{1,0:T(8,128)} %get-tuple-element.168, f32[1024,512]{1,0:T(8,128)S(1)} %copy-done, f32[1600,1024]{1,0:T(8,128)} %get-tuple-element.143, f32[1600,1024]{1,0:T(8,128)} %get-tuple-element.142), kind=kOutput, calls=%fused_computation.23 | convolution fusion | flops 40278622208 | bytes 22675456 | tf_op jit(solution)/shard_map/dot_general | solution.py:93
  649.0 7.4 convert_element_type.106
  656.3 2.4 copy.25
  658.7 13.0 %copy.21 = bf16[64,25,2,512]{0,1,2,3:T(8,128)(2,1)} copy(bf16[64,25,2,512]{3,2,1,0:T(2,128)(2,1)S(1)} %convert_element_type.106) | data formatting | bytes 6553600 | tf_op jit(solution)/shard_map/convert_element_type | solution.py:97
  671.7 2.1 fusion.40
  673.9 0.3 maximum_bitcast_fusion
  674.2 5.3 pad_maximum_fusion
  679.5 23.9 %copy.12 = bf16[2,2,64,25,512]{2,3,1,0,4:T(8,128)(2,1)} copy(bf16[2,2,64,25,512]{4,2,3,1,0:T(8,128)(2,1)} %pad_maximum_fusion) | data formatting | bytes 13107200 | tf_op jit(solution)/shard_map/stack | solution.py:98
  703.4 20.9 %fusion = f32[2,64,1,64,512]{1,3,0,4,2:T(8,128)} fusion(bf16[2,2,64,25,512]{2,3,1,0,4:T(8,128)(2,1)} %copy.12, bf16[64,25,2,512]{0,1,2,3:T(8,128)(2,1)} %copy.21), kind=kOutput, calls=%fused_computation.3 | convolution fusion | flops 423624704 | bytes 26607616 | tf_op jit(solution)/shard_map/opisc,pmsc->oimc/dot_general | solution.py:58
  724.3 63.0 %scatter.4 = f32[2,64,5,64,512]{1,3,0,4,2:T(8,128)} pad(f32[2,64,1,64,512]{1,3,0,4,2:T(8,128)} %fusion, f32[]{:T(128)} %constant.152.clone.1), padding=0_0x0_0x0_4x0_0x0_0 | pad | bytes 100663296 | tf_op jit(solution)/shard_map/scatter | solution.py:100
  787.3 297.2 %while.18 = (s32[]{:T(128)}, bf16[2,64,25,512]{3,1,2,0:T(8,128)(2,1)}, f32[2,64,5,64,512]{1,3,0,4,2:T(8,128)}, bf16[2,2,64,25,512]{2,3,1,0,4:T(8,128)(2,1)}, s32[]{:T(128)}, /*index=5*/s32[]{:T(128)}, s32[]{:T(128)}) while((s32[]{:T(128)}, bf16[2,64,25,512]{3,1,2,0:T(8,128)(2,1)}, f32[2,64,5,64,512]{1,3,0,4,2:T(8,128)}, ...), condition=%wide.region_3.4_spmd, body=%wide.region_2.3_spmd.sunk | while | flops 423624704 | bytes 84934808 | solution.py:109
  787.3 1.2 collective-permute-start
  788.5 36.5 %collective-permute-done = bf16[2,64,25,512]{3,1,2,0:T(8,128)(2,1)S(1)} collective-permute-done((bf16[2,64,25,512]{3,1,2,0:T(8,128)(2,1)}, bf16[2,64,25,512]{3,1,2,0:T(8,128)(2,1)S(1)}, u32[]{:S(2)}, u32[]{:S(2)}) %collective-permute-start) | collective-permute-done | bytes 3276832 | tf_op jit(solution)/shard_map/while/body/eval_jaxpr/ppermute | solution.py:13
  825.1 12.5 %copy.27 = bf16[2,64,25,512,1]{1,2,0,4,3:T(8,128)(2,1)} copy(bf16[2,64,25,512,1]{3,1,2,0,4:T(8,128)(2,1)S(1)} %bitcast.67) | data formatting | bytes 6553600 | tf_op jit(solution)/shard_map/while/body/eval_jaxpr/ppermute | solution.py:13
  837.5 20.6 %bitcast_dynamic-update-slice_fusion.2 = f32[2,64,5,64,512]{1,3,0,4,2:T(8,128)} fusion(f32[2,64,5,64,512]{1,3,0,4,2:T(8,128)} %get-tuple-element.204, s32[]{:T(128)S(6)} %select_n.115, bf16[2,64,25,512,1]{1,2,0,4,3:T(8,128)(2,1)} %copy.27, bf16[2,2,64,25,512]{2,3,1,0,4:T(8,128)(2,1)} %get-tuple-element.212), kind=kOutput, calls=%fused_computation.clone.1 | convolution fusion | flops 423624704 | bytes 58720260 | tf_op jit(solution)/shard_map/while/body/eval_jaxpr/opisc,pmsc->oimc/dot_general | solution.py:58
  858.2 1.6 copy.40
  859.8 3.6 collective-permute-start
  863.4 36.5 %collective-permute-done = bf16[2,64,25,512]{3,1,2,0:T(8,128)(2,1)S(1)} collective-permute-done((bf16[2,64,25,512]{3,1,2,0:T(8,128)(2,1)}, bf16[2,64,25,512]{3,1,2,0:T(8,128)(2,1)S(1)}, u32[]{:S(2)}, u32[]{:S(2)}) %collective-permute-start) | collective-permute-done | bytes 3276832 | tf_op jit(solution)/shard_map/while/body/eval_jaxpr/ppermute | solution.py:13
  899.9 12.5 %copy.27 = bf16[2,64,25,512,1]{1,2,0,4,3:T(8,128)(2,1)} copy(bf16[2,64,25,512,1]{3,1,2,0,4:T(8,128)(2,1)S(1)} %bitcast.67) | data formatting | bytes 6553600 | tf_op jit(solution)/shard_map/while/body/eval_jaxpr/ppermute | solution.py:13
  912.4 20.8 %bitcast_dynamic-update-slice_fusion.2 = f32[2,64,5,64,512]{1,3,0,4,2:T(8,128)} fusion(f32[2,64,5,64,512]{1,3,0,4,2:T(8,128)} %get-tuple-element.204, s32[]{:T(128)S(6)} %select_n.115, bf16[2,64,25,512,1]{1,2,0,4,3:T(8,128)(2,1)} %copy.27, bf16[2,2,64,25,512]{2,3,1,0,4:T(8,128)(2,1)} %get-tuple-element.212), kind=kOutput, calls=%fused_computation.clone.1 | convolution fusion | flops 423624704 | bytes 58720260 | tf_op jit(solution)/shard_map/while/body/eval_jaxpr/opisc,pmsc->oimc/dot_general | solution.py:58
  933.1 1.6 copy.40
  934.8 3.6 collective-permute-start
  938.4 36.5 %collective-permute-done = bf16[2,64,25,512]{3,1,2,0:T(8,128)(2,1)S(1)} collective-permute-done((bf16[2,64,25,512]{3,1,2,0:T(8,128)(2,1)}, bf16[2,64,25,512]{3,1,2,0:T(8,128)(2,1)S(1)}, u32[]{:S(2)}, u32[]{:S(2)}) %collective-permute-start) | collective-permute-done | bytes 3276832 | tf_op jit(solution)/shard_map/while/body/eval_jaxpr/ppermute | solution.py:13
  974.9 12.5 %copy.27 = bf16[2,64,25,512,1]{1,2,0,4,3:T(8,128)(2,1)} copy(bf16[2,64,25,512,1]{3,1,2,0,4:T(8,128)(2,1)S(1)} %bitcast.67) | data formatting | bytes 6553600 | tf_op jit(solution)/shard_map/while/body/eval_jaxpr/ppermute | solution.py:13
  987.3 20.6 %bitcast_dynamic-update-slice_fusion.2 = f32[2,64,5,64,512]{1,3,0,4,2:T(8,128)} fusion(f32[2,64,5,64,512]{1,3,0,4,2:T(8,128)} %get-tuple-element.204, s32[]{:T(128)S(6)} %select_n.115, bf16[2,64,25,512,1]{1,2,0,4,3:T(8,128)(2,1)} %copy.27, bf16[2,2,64,25,512]{2,3,1,0,4:T(8,128)(2,1)} %get-tuple-element.212), kind=kOutput, calls=%fused_computation.clone.1 | convolution fusion | flops 423624704 | bytes 58720260 | tf_op jit(solution)/shard_map/while/body/eval_jaxpr/opisc,pmsc->oimc/dot_general | solution.py:58
  1008.0 1.6 copy.40
  1009.6 3.6 collective-permute-start
  1013.2 36.5 %collective-permute-done = bf16[2,64,25,512]{3,1,2,0:T(8,128)(2,1)S(1)} collective-permute-done((bf16[2,64,25,512]{3,1,2,0:T(8,128)(2,1)}, bf16[2,64,25,512]{3,1,2,0:T(8,128)(2,1)S(1)}, u32[]{:S(2)}, u32[]{:S(2)}) %collective-permute-start) | collective-permute-done | bytes 3276832 | tf_op jit(solution)/shard_map/while/body/eval_jaxpr/ppermute | solution.py:13
  1049.7 12.5 %copy.27 = bf16[2,64,25,512,1]{1,2,0,4,3:T(8,128)(2,1)} copy(bf16[2,64,25,512,1]{3,1,2,0,4:T(8,128)(2,1)S(1)} %bitcast.67) | data formatting | bytes 6553600 | tf_op jit(solution)/shard_map/while/body/eval_jaxpr/ppermute | solution.py:13
  1062.2 20.7 %bitcast_dynamic-update-slice_fusion.2 = f32[2,64,5,64,512]{1,3,0,4,2:T(8,128)} fusion(f32[2,64,5,64,512]{1,3,0,4,2:T(8,128)} %get-tuple-element.204, s32[]{:T(128)S(6)} %select_n.115, bf16[2,64,25,512,1]{1,2,0,4,3:T(8,128)(2,1)} %copy.27, bf16[2,2,64,25,512]{2,3,1,0,4:T(8,128)(2,1)} %get-tuple-element.212), kind=kOutput, calls=%fused_computation.clone.1 | convolution fusion | flops 423624704 | bytes 58720260 | tf_op jit(solution)/shard_map/while/body/eval_jaxpr/opisc,pmsc->oimc/dot_general | solution.py:58
  1082.9 1.6 copy.40
  1084.5 124.9 %copy.14 = f32[2,64,5,64,512]{4,3,2,1,0:T(8,128)} copy(f32[2,64,5,64,512]{1,3,0,4,2:T(8,128)} %get-tuple-element.127) | data formatting | bytes 167772160 | tf_op jit(solution)/shard_map/while | solution.py:109
Async XLA Ops:
  0.0 234.7 %collective-permute-start.2 = (bf16[64,40960]{1,0:T(8,128)(2,1)}, bf16[64,40960]{1,0:T(8,128)(2,1)}, u32[]{:S(2)}, u32[]{:S(2)}) collective-permute-start(bf16[64,40960]{1,0:T(8,128)(2,1)} %param.6), channel_id=1, source_target_pairs={{0,24},{8,0},{16,8},{24,16},{1,25},{9,1},{17,9},{25,17},{2,26},{10... | collective-permute-start | bytes 15728648 | tf_op jit(solution)/shard_map/ppermute | solution.py:87
  3.9 226.0 %collective-permute-start.1 = (bf16[64,40960]{1,0:T(8,128)(2,1)}, bf16[64,40960]{1,0:T(8,128)(2,1)}, u32[]{:S(2)}, u32[]{:S(2)}) collective-permute-start(bf16[64,40960]{1,0:T(8,128)(2,1)} %param.6), channel_id=1, source_target_pairs={{0,8},{8,16},{16,24},{24,0},{1,9},{9,17},{17,25},{25,1},{2,10},{10... | collective-permute-start | bytes 15728648 | tf_op jit(solution)/shard_map/ppermute | solution.py:82
  21.7 4.9 copy-start.1
  229.9 115.1 %collective-permute-start.3 = (bf16[64,40960]{1,0:T(8,128)(2,1)}, bf16[64,40960]{1,0:T(8,128)(2,1)}, u32[]{:S(2)}, u32[]{:S(2)}) collective-permute-start(bf16[64,40960]{1,0:T(8,128)(2,1)} %collective-permute-done.1), channel_id=1, source_target_pairs={{0,8},{8,16},{16,24},{24,0},{1,9},{9,17},{17,25},{25,1},{2,10},{10... | collective-permute-start | bytes 15728648 | tf_op jit(solution)/shard_map/ppermute | solution.py:82
  587.4 13.1 %copy-start = (f32[1024,512]{1,0:T(8,128)S(1)}, f32[1024,512]{1,0:T(8,128)}, u32[]{:S(2)}) copy-start(f32[1024,512]{1,0:T(8,128)} %fusion.24) | copy-start | bytes 6291460
  787.3 37.8 %collective-permute-start = (bf16[2,64,25,512]{3,1,2,0:T(8,128)(2,1)}, bf16[2,64,25,512]{3,1,2,0:T(8,128)(2,1)S(1)}, u32[]{:S(2)}, u32[]{:S(2)}) collective-permute-start(bf16[2,64,25,512]{3,1,2,0:T(8,128)(2,1)} %get-tuple-element.203), channel_id=1, source_target_pairs={{0,7},{1,0},{2,1},{3,2},{4,3},{5,4},{6,5},{7,6},{8,15},{9,8},{10,9... | collective-permute-start | bytes 9830408 | tf_op jit(solution)/shard_map/while/body/eval_jaxpr/ppermute | solution.py:13
  859.8 40.1 %collective-permute-start = (bf16[2,64,25,512]{3,1,2,0:T(8,128)(2,1)}, bf16[2,64,25,512]{3,1,2,0:T(8,128)(2,1)S(1)}, u32[]{:S(2)}, u32[]{:S(2)}) collective-permute-start(bf16[2,64,25,512]{3,1,2,0:T(8,128)(2,1)} %get-tuple-element.203), channel_id=1, source_target_pairs={{0,7},{1,0},{2,1},{3,2},{4,3},{5,4},{6,5},{7,6},{8,15},{9,8},{10,9... | collective-permute-start | bytes 9830408 | tf_op jit(solution)/shard_map/while/body/eval_jaxpr/ppermute | solution.py:13
  934.8 40.1 %collective-permute-start = (bf16[2,64,25,512]{3,1,2,0:T(8,128)(2,1)}, bf16[2,64,25,512]{3,1,2,0:T(8,128)(2,1)S(1)}, u32[]{:S(2)}, u32[]{:S(2)}) collective-permute-start(bf16[2,64,25,512]{3,1,2,0:T(8,128)(2,1)} %get-tuple-element.203), channel_id=1, source_target_pairs={{0,7},{1,0},{2,1},{3,2},{4,3},{5,4},{6,5},{7,6},{8,15},{9,8},{10,9... | collective-permute-start | bytes 9830408 | tf_op jit(solution)/shard_map/while/body/eval_jaxpr/ppermute | solution.py:13
  1009.6 40.1 %collective-permute-start = (bf16[2,64,25,512]{3,1,2,0:T(8,128)(2,1)}, bf16[2,64,25,512]{3,1,2,0:T(8,128)(2,1)S(1)}, u32[]{:S(2)}, u32[]{:S(2)}) collective-permute-start(bf16[2,64,25,512]{3,1,2,0:T(8,128)(2,1)} %get-tuple-element.203), channel_id=1, source_target_pairs={{0,7},{1,0},{2,1},{3,2},{4,3},{5,4},{6,5},{7,6},{8,15},{9,8},{10,9... | collective-permute-start | bytes 9830408 | tf_op jit(solution)/shard_map/while/body/eval_jaxpr/ppermute | solution.py:13
